TPU v7x, 32 devices: a whole 2x2x4 slice. The times are simulated.
32 devices in a mesh: row: 4 (over y, x), col: 8 (over z, core).
Axes of the slice: x: 2, y: 2, z: 4, core: 2. Of those that a mesh axis runs over, the one named last changes fastest.
Arguments:
- positions: float32 [3, 4096], P(None, ('row', 'col')), may hold values from 0 to 5
- species: int32 [4096], P(('row', 'col')), may hold values from 0 to 99
- tile_list: int32 [4, 8, 2, 3], P('row', 'col'), may hold values from 0 to 7, as said below
- pair_mask: int32 [4, 8, 2, 128, 128], P('row', 'col'), may hold values 0 or 1
- embed: float32 [100, 128], replicated, may hold values from -6 to 6
- w_in: float32 [2, 128, 128], replicated, may hold values from -0.5 to 0.5
- rbf_weight: bfloat16 [2, 256, 128], replicated, may hold values from -1 to 1
- rbf_bias: float32 [2, 128], replicated, may hold values from -4 to 4
- filt_weight: bfloat16 [2, 128, 128], replicated, may hold values from -1 to 1
- w_update1: float32 [2, 128, 128], replicated, may hold values from -1 to 1
- w_update2: float32 [2, 128, 128], replicated, may hold values from -0.5 to 0.5
- w_out1: float32 [128, 64], replicated, may hold values from -0.5 to 0.5
- w_out2: float32 [64], replicated, may hold values from -0.75 to 0.75
Outputs:
- atom_energy: float32 [4096], P(('row', 'col'))
- forces: float32 [3, 4096], P(None, ('row', 'col'))
Inputs may be any that keep to these rules, and one draw needn't show every extreme that they name: `tile_list`: A live slot (flag 1) names a row block below 8 and a column block below 4; the live slots of one device name distinct row blocks and come first; a dead slot is all zeros; every device has at least one live slot and some device has all 2.
All inputs are finite; a program needn't handle non-finite values. No bound on the sum of `pair_mask` on one device may be relied on, other than what follows from the above.
Results may differ from a plain program's by a relative error of at most 0.007.
Values sent between devices are 32-bit elements; how exact they have to be, the bound alone decides.
A program may use at most 192 MiB of HBM per device.

v0:
```python
from functools import partial
import math

import jax
import jax.numpy as jnp
from jax import lax
from jax.experimental import pallas as pl
from jax.experimental.pallas import tpu as pltpu
from jax.sharding import PartitionSpec as P

CUTOFF = 5.0
NORM_DIV = 4.0
HIGH = lax.Precision.HIGHEST
MESH = pl.DeviceIdType.MESH
GROUP = 8
SUB = 4
F32 = jnp.float32
BF16 = jnp.bfloat16


def ssp_parts(values):
    th = jnp.tanh(0.5 * values)
    return jnp.maximum(values, 0.0) - jnp.log(1.0 + jnp.abs(th)), 0.5 * (1.0 + th)


def dot_nn(a, b):
    return lax.dot_general(a, b, (((1,), (0,)), ((), ())), precision=HIGH, preferred_element_type=F32)


def dot_nt(a, b):
    return lax.dot_general(a, b, (((1,), (1,)), ((), ())), precision=HIGH, preferred_element_type=F32)


def kernel(
    n_row, n_col, slots,
    tl, pos, spec, mask, embed, w_in, rbf_w, rbf_b, filt_w, wu1, wu2, wo1, wo2,
    e_out, f_out,
    posblk, rowpos, colpos, emb_s, wc, fc,
    ubuf, envb, envp, unit, es, ds, hs, ts,
    g1_s, dg_s, msg, sibmsg, sbuf, rbuf, xbuf0, xbuf1, gbuf0, gbuf1, dxs, dxsend, dxrecv,
    st, rfsend, rfrecv, cfsend, cfrecv,
    send_sem, recv_sem,
):
    blk = pos.shape[1]
    feat = w_in.shape[2]
    n_gauss = rbf_w.shape[1]
    nz = n_col // 2
    me_r = lax.axis_index("row")
    me_c = lax.axis_index("col")
    z = me_c // 2
    core = me_c % 2
    sib = z * 2 + (1 - core)
    started = []
    xbuf, gbuf = (xbuf0, xbuf1), (gbuf0, gbuf1)

    def send(src, dst, r, c):
        n = len(started)
        copy = pltpu.make_async_remote_copy(
            src_ref=src, dst_ref=dst, send_sem=send_sem.at[n], recv_sem=recv_sem.at[n],
            device_id=(r, c), device_id_type=MESH)
        copy.start()
        started.append(copy)
        return copy

    row_peers = [(lax.rem(me_r + o, n_row), me_c) for o in range(1, n_row)]
    col_peers = [(me_r, lax.rem(me_c + o, n_col)) for o in range(1, n_col)]
    same_peers = [lax.rem(z + o, nz) for o in range(1, nz)]

    barrier = pltpu.get_barrier_semaphore()
    for peer in row_peers + col_peers:
        pl.semaphore_signal(barrier, inc=1, device_id=peer, device_id_type=MESH)

    posblk[...] = jnp.zeros_like(posblk)
    posblk[0:3, :] = pos[...]
    for k in range(slots):
        posblk[3 + k:4 + k, :] = jnp.full((1, blk), tl[0, 0, k, 0], jnp.int32).astype(F32)
        posblk[3 + slots + k:4 + slots + k, :] = jnp.full((1, blk), tl[0, 0, k, 1], jnp.int32).astype(F32)
    rowpos[me_c] = posblk[...]
    colpos[me_r] = posblk[...]

    pl.semaphore_wait(barrier, len(row_peers) + len(col_peers))
    pos_copies = [send(posblk, rowpos.at[me_c], *peer) for peer in col_peers]
    pos_copies += [send(posblk, colpos.at[me_r], *peer) for peer in row_peers]

    emb_s[...] = jnp.zeros_like(emb_s)
    emb_s[0:embed.shape[0], :] = embed[...]
    onehot_t = (lax.broadcasted_iota(jnp.int32, (blk, blk), 0) == spec[...]).astype(F32)
    features = dot_nn(onehot_t.T, emb_s[...])

    def gather_features(layer, value):
        xbuf[layer][me_r] = value
        return [send(xbuf[layer].at[me_r], xbuf[layer].at[me_r], *peer) for peer in row_peers]

    x_copies = gather_features(0, dot_nn(features, w_in[0]))

    wc[:, 0:feat] = (rbf_w[0].astype(F32) * 0.5).astype(BF16)
    wc[:, feat:2 * feat] = (rbf_w[1].astype(F32) * 0.5).astype(BF16)
    fc[...] = jnp.zeros_like(fc)
    fc[0:feat, 0:feat] = (filt_w[0].astype(F32) * 2.0).astype(BF16)
    fc[feat:2 * feat, feat:2 * feat] = (filt_w[1].astype(F32) * 2.0).astype(BF16)
    bias = 0.5 * jnp.concatenate([rbf_b[0:1, :], rbf_b[1:2, :]], axis=1)

    sharp = (n_gauss / CUTOFF) ** 2 / 32.0
    alpha = math.sqrt(sharp / math.log(2.0))
    centers = lax.broadcasted_iota(jnp.int32, (1, n_gauss), 1).astype(F32) * (alpha * CUTOFF / n_gauss)
    half_kappa = -math.log(2.0) * alpha

    for copy in pos_copies:
        copy.wait_recv()

    rows = [tl[0, 0, k, 0] for k in range(slots)]
    cols = [tl[0, 0, k, 1] for k in range(slots)]
    for k in range(slots):
        rp = rowpos[rows[k]]
        cp = colpos[cols[k]]
        diffs = []
        for a in range(3):
            pj = jnp.broadcast_to(cp[a:a + 1, :], (blk, blk)).T
            diffs.append(rp[a:a + 1, :] - pj)
        dist = jnp.sqrt(diffs[0] * diffs[0] + diffs[1] * diffs[1] + diffs[2] * diffs[2] + 0.01)
        inv = 1.0 / dist
        for a in range(3):
            unit[k, a] = diffs[a] * inv
        gate = (mask[0, 0, k] * tl[0, 0, k, 2]).astype(F32).T * (1.0 / NORM_DIV)
        near = jnp.where(dist < CUTOFF, gate, 0.0)
        phase = dist * (math.pi / CUTOFF)
        ubuf[k] = dist * alpha
        envb[k] = 0.5 * (jnp.cos(phase) + 1.0) * near
        envp[k] = (-0.5 * math.pi / CUTOFF) * jnp.sin(phase) * near

    for copy in x_copies:
        copy.wait_recv()

    def filter_group(k, step, x0):
        first = step * GROUP
        shift = lax.rem(blk - first, blk)
        ur = pltpu.roll(ubuf[k], shift, 1)
        er = pltpu.roll(envb[k], shift, 1)
        pr = pltpu.roll(envp[k], shift, 1)
        msg_rows = []
        for half in range(GROUP // SUB):
            for a in range(SUB):
                lane = half * SUB + a
                t = ur[:, lane:lane + 1] - centers
                e = jnp.exp2(-(t * t))
                es[half, a * blk:(a + 1) * blk, :] = e.astype(BF16)
                ds[half, a * blk:(a + 1) * blk, :] = (t * e).astype(BF16)
            pre = jnp.dot(es[half], wc[...], preferred_element_type=F32) + bias
            th = jnp.tanh(pre)
            hs[half] = (jnp.maximum(pre, 0.0) - 0.5 * jnp.log(1.0 + jnp.abs(th))).astype(BF16)
            ts[half] = ((1.0 + th) * jnp.dot(ds[half], wc[...], preferred_element_type=F32)).astype(BF16)
            filt = jnp.dot(hs[half], fc[...], preferred_element_type=F32)
            dfilt = jnp.dot(ts[half], fc[...], preferred_element_type=F32)
            for a in range(SUB):
                lane = half * SUB + a
                fa = filt[a * blk:(a + 1) * blk, :]
                da = dfilt[a * blk:(a + 1) * blk, :]
                e = er[:, lane:lane + 1]
                p = pr[:, lane:lane + 1]
                gv = fa * e
                msg_rows.append(jnp.sum(gv[:, 0:feat] * x0, axis=0, keepdims=True))
                g1_s[k, first + lane] = gv[:, feat:2 * feat].astype(BF16)
                dg_s[k, first + lane] = (da * (e * half_kappa) + fa * p).astype(BF16)
        msg[0, k, pl.ds(pl.multiple_of(first, GROUP), GROUP), :] = jnp.concatenate(msg_rows, axis=0)

    for k in range(slots):
        x0 = xbuf[0][cols[k]]

        def filter_step(step, carry, k=k, x0=x0):
            filter_group(k, step, x0)
            return carry

        lax.fori_loop(0, blk // GROUP, filter_step, 0)

    def reduce_messages(layer):
        to_sib = send(msg.at[layer], sibmsg.at[layer], me_r, sib)
        own_rows = posblk[...]
        sib_rows = rowpos[sib]
        to_sib.wait_recv()

        def share(zz):
            dest = (zz * 2 + core).astype(F32)
            total = None
            for k in range(slots):
                part = jnp.where(own_rows[3 + k:4 + k, :] == dest, 1.0, 0.0) * msg[layer, k]
                part += jnp.where(sib_rows[3 + k:4 + k, :] == dest, 1.0, 0.0) * sibmsg[layer, k]
                total = part if total is None else total + part
            return total

        copies = []
        for o, zz in enumerate(same_peers):
            sbuf[layer, o] = share(zz)
            copies.append(send(sbuf.at[layer, o], rbuf.at[layer, o], me_r, zz * 2 + core))
        total = share(z)
        for o, copy in enumerate(copies):
            copy.wait_recv()
            total = total + rbuf[layer, o]
        return total

    def gather_cotangents(layer, value):
        gbuf[layer][me_c] = value
        mine = gbuf[layer].at[me_c]
        across = [send(mine, mine, me_r, zz * 2 + core) for zz in same_peers]
        local = [send(mine, mine, me_r, sib)]
        return across, local

    def finish_cotangents(layer, across, local):
        for o, copy in enumerate(across):
            copy.wait_recv()
            source = lax.rem(z + nz - (o + 1), nz) * 2 + core
            block = gbuf[layer].at[source]
            local.append(send(block, block, me_r, sib))
        for copy in local:
            copy.wait_recv()

    message = reduce_messages(0)
    act, sig0 = ssp_parts(dot_nn(message, wu1[0]))
    features = features + dot_nn(act, wu2[0])
    x_copies = gather_features(1, dot_nn(features, w_in[1]))
    for copy in x_copies:
        copy.wait_recv()

    for k in range(slots):
        x1 = xbuf[1][cols[k]]

        def message_step(step, carry, k=k, x1=x1):
            first = step * GROUP
            parts = [
                jnp.sum(g1_s[k, first + a].astype(F32) * x1, axis=0, keepdims=True)
                for a in range(GROUP)
            ]
            msg[1, k, pl.ds(pl.multiple_of(first, GROUP), GROUP), :] = jnp.concatenate(parts, axis=0)
            return carry

        lax.fori_loop(0, blk // GROUP, message_step, 0)

    message = reduce_messages(1)
    act, sig1 = ssp_parts(dot_nn(message, wu1[1]))
    features = features + dot_nn(act, wu2[1])

    act, sig_out = ssp_parts(dot_nn(features, wo1[...]))
    e_out[...] = dot_nt(jnp.broadcast_to(wo2[...], (8, wo2.shape[1])), act)[0:1, :]
    grad_feat = dot_nt(sig_out * wo2[...], wo1[...])

    grad_msg = dot_nt(dot_nt(grad_feat, wu2[1]) * sig1, wu1[1])
    across, local = gather_cotangents(1, grad_msg)
    finish_cotangents(1, across, local)

    for k in range(slots):
        def dx_step(step, acc, k=k):
            first = pl.multiple_of(step * GROUP, GROUP)
            gr = gbuf[1][rows[k], pl.ds(first, GROUP), :]
            for a in range(GROUP):
                acc = acc + g1_s[k, first + a].astype(F32) * gr[a:a + 1, :]
            return acc

        dxs[k] = lax.fori_loop(0, blk // GROUP, dx_step, jnp.zeros((blk, feat), F32))

    own_cols = posblk[...]

    def dx_share(dest):
        total = None
        for k in range(slots):
            part = jnp.where(own_cols[3 + slots + k:4 + slots + k, :] == dest.astype(F32), 1.0, 0.0) * dxs[k]
            total = part if total is None else total + part
        return total

    dx_copies = []
    for o, (r, c) in enumerate(row_peers):
        dxsend[o] = dx_share(r)
        dx_copies.append(send(dxsend.at[o], dxrecv.at[o], r, c))
    grad_in = dx_share(me_r)

    lane_id = lax.broadcasted_iota(jnp.int32, (blk, blk), 1)

    def pair_slopes(layer, k, begin):
        xk = xbuf[layer][cols[k]]

        def slope_step(step, acc):
            first = pl.multiple_of(step * GROUP, GROUP)
            gr = gbuf[layer][rows[k], pl.ds(first, GROUP), :]
            for a in range(GROUP):
                dg = dg_s[k, first + a, :, layer * feat:(layer + 1) * feat].astype(F32)
                red = jnp.sum(dg * (xk * gr[a:a + 1, :]), axis=1, keepdims=True)
                acc = jnp.where(lane_id == first + a, acc + red, acc)
            return acc

        return lax.fori_loop(0, blk // GROUP, slope_step, begin)

    for o, copy in enumerate(dx_copies):
        copy.wait_recv()
        grad_in = grad_in + dxrecv[o]
    grad_feat = grad_feat + dot_nt(grad_in, w_in[1])
    grad_msg = dot_nt(dot_nt(grad_feat, wu2[0]) * sig0, wu1[0])
    across, local = gather_cotangents(0, grad_msg)
    for k in range(slots):
        st[k] = pair_slopes(1, k, jnp.zeros((blk, blk), F32))
    finish_cotangents(0, across, local)

    row_force, col_force = [], []
    for k in range(slots):
        slope = pair_slopes(0, k, st[k])
        rf, cf = [], []
        for a in range(3):
            pull = slope * unit[k, a]
            rf.append(jnp.sum(pull, axis=0, keepdims=True))
            cf.append(-jnp.sum(pull.T, axis=0, keepdims=True))
        pad = jnp.zeros((5, blk), F32)
        row_force.append(jnp.concatenate(rf + [pad], axis=0))
        col_force.append(jnp.concatenate(cf + [pad], axis=0))

    def force_share(parts, base, dest):
        total = None
        for k in range(slots):
            part = jnp.where(own_cols[base + k:base + k + 1, :] == dest.astype(F32), 1.0, 0.0) * parts[k]
            total = part if total is None else total + part
        return total

    copies = []
    for o, (r, c) in enumerate(col_peers):
        rfsend[o] = force_share(row_force, 3, c)
        copies.append((send(rfsend.at[o], rfrecv.at[o], r, c), rfrecv, o))
    for o, (r, c) in enumerate(row_peers):
        cfsend[o] = force_share(col_force, 3 + slots, r)
        copies.append((send(cfsend.at[o], cfrecv.at[o], r, c), cfrecv, o))
    total = force_share(row_force, 3, me_c) + force_share(col_force, 3 + slots, me_r)
    for copy, ref, o in copies:
        copy.wait_recv()
        total = total + ref[o]
    f_out[...] = -total[0:3, :]
    for copy in started:
        copy.wait_send()


def body(n_row, n_col, positions, species, tile_list, pair_mask, embed, w_in, rbf_weight, rbf_bias,
         filt_weight, w_update1, w_update2, w_out1, w_out2):
    blk = positions.shape[1]
    feat = embed.shape[1]
    slots = tile_list.shape[2]
    n_gauss = rbf_weight.shape[1]
    nz = n_col // 2
    n_sems = (
        (n_col - 1 + n_row - 1) * 2 + 2 * (n_row - 1) + 2 * (1 + nz - 1)
        + 2 * (2 * nz - 1) + (n_row - 1)
    )
    vm = pltpu.VMEM
    sub = SUB * blk
    scratch = [
        vm((8, blk), F32), vm((n_col, 8, blk), F32), vm((n_row, 8, blk), F32),
        vm((blk, feat), F32), vm((n_gauss, 2 * feat), BF16), vm((2 * feat, 2 * feat), BF16),
        vm((slots, blk, blk), F32), vm((slots, blk, blk), F32), vm((slots, blk, blk), F32),
        vm((slots, 3, blk, blk), F32),
        vm((GROUP // SUB, sub, n_gauss), BF16), vm((GROUP // SUB, sub, n_gauss), BF16),
        vm((GROUP // SUB, sub, 2 * feat), BF16), vm((GROUP // SUB, sub, 2 * feat), BF16),
        vm((slots, blk, blk, feat), BF16), vm((slots, blk, blk, 2 * feat), BF16),
        vm((2, slots, blk, feat), F32), vm((2, slots, blk, feat), F32),
        vm((2, nz - 1, blk, feat), F32), vm((2, nz - 1, blk, feat), F32),
        vm((n_row, blk, feat), F32), vm((n_row, blk, feat), F32),
        vm((n_col, blk, feat), F32), vm((n_col, blk, feat), F32),
        vm((slots, blk, feat), F32),
        vm((n_row - 1, blk, feat), F32), vm((n_row - 1, blk, feat), F32),
        vm((slots, blk, blk), F32),
        vm((n_col - 1, 8, blk), F32), vm((n_col - 1, 8, blk), F32),
        vm((n_row - 1, 8, blk), F32), vm((n_row - 1, 8, blk), F32),
        pltpu.SemaphoreType.DMA((n_sems,)), pltpu.SemaphoreType.DMA((n_sems,)),
    ]
    vspec = pl.BlockSpec(memory_space=pltpu.VMEM)
    energies, forces = pl.pallas_call(
        partial(kernel, n_row, n_col, slots),
        out_shape=(jax.ShapeDtypeStruct((1, blk), F32), jax.ShapeDtypeStruct((3, blk), F32)),
        in_specs=[pl.BlockSpec(memory_space=pltpu.SMEM)] + [vspec] * 12,
        out_specs=(vspec, vspec),
        scratch_shapes=scratch,
        compiler_params=pltpu.CompilerParams(
            collective_id=0, has_side_effects=True, vmem_limit_bytes=56 * 1024 * 1024),
    )(tile_list, positions, species.reshape(1, blk), pair_mask, embed, w_in, rbf_weight, rbf_bias,
      filt_weight, w_update1, w_update2, w_out1, w_out2.reshape(1, w_out2.shape[0]))
    return energies.reshape(blk), forces


def solution(mesh):
    n_row, n_col = mesh.shape["row"], mesh.shape["col"]
    return jax.shard_map(
        partial(body, n_row, n_col),
        mesh=mesh,
        in_specs=(
            P(None, ("row", "col")),
            P(("row", "col")),
            P("row", "col", None, None),
            P("row", "col", None, None, None),
            P(), P(), P(), P(), P(), P(), P(), P(), P(),
        ),
        out_specs=(P(("row", "col")), P(None, ("row", "col"))),
        check_vma=False,
    )
```

profile of v0, /device:TPU:0, one launch (start us, length us, event | category | flops | bytes accessed | tf_op | source)
XLA Modules:
  0.0 115.6 jit_solution(4074747455755479110)
XLA Ops:
  0.6 1.5 %copy.15.wo1 = f32[128,64]{1,0:T(8,128)} copy(f32[128,64]{0,1:T(8,128)} %param.24) | data formatting | bytes 65536 | tf_op args[11]
  2.1 111.8 %shard_map.140 = (f32[1,128]{1,0:T(1,128)}, f32[3,128]{1,0:T(4,128)}) custom-call(s32[1,1,2,3]{3,2,1,0:T(2,128)} %tl.1, f32[3,128]{1,0:T(4,128)} %pos.1, s32[1,128]{1,0:T(1,128)} %bitcast.3, s32[1,1,2,128,128]{4,3,2,1,0:T(8,128)} %mask.1, f32[100,128]{1,0:T(8,128)} %embed.1, f32[2,128,128]{2,1,0:T(8,128)} %w_in.1, bf16[2,256,128]{2,1,0:T(8,128)(2,1)} %rbf_w.1, ...), custom_call_target="tpu_custom_call" | custom-call | tf_op jit(solution)/shard_map/pallas_call | solution.py:368
  113.9 0.0 copy-start.1
  113.9 0.0 copy-start
  113.9 0.6 copy-done.1
  114.5 0.5 copy.18
  115.0 0.0 copy-done
  115.0 0.6 copy.19
Async XLA Ops:
  113.9 0.6 copy-start.1
  113.9 1.1 copy-start
where the time goes:
time: 116 us
  Pallas kernels  112 us (97%)
  local copies, waits for them, and re-layouts  3.14 us (3%)
    pallas_call x1, Pallas kernels, body(): pl.pallas_call(partial(kernel, n_row, n_col, slots), out_shape=(jax.Shape...  112 us
    unnamed x7, local copies, waits for them, and re-layouts  3.14 us

commit v1 on v0

--- a/solution.py
+++ b/solution.py
@@ -131,12 +131,12 @@
     for copy in x_copies:
         copy.wait_recv()
 
-    def filter_group(k, step, x0):
+    def filter_group(k, step, x0, forward, slope):
         first = step * GROUP
         shift = lax.rem(blk - first, blk)
         ur = pltpu.roll(ubuf[k], shift, 1)
         er = pltpu.roll(envb[k], shift, 1)
-        pr = pltpu.roll(envp[k], shift, 1)
+        pr = pltpu.roll(envp[k], shift, 1) if slope else None
         msg_rows = []
         for half in range(GROUP // SUB):
             for a in range(SUB):
@@ -144,39 +144,62 @@
                 t = ur[:, lane:lane + 1] - centers
                 e = jnp.exp2(-(t * t))
                 es[half, a * blk:(a + 1) * blk, :] = e.astype(BF16)
-                ds[half, a * blk:(a + 1) * blk, :] = (t * e).astype(BF16)
+                if slope:
+                    ds[half, a * blk:(a + 1) * blk, :] = (t * e).astype(BF16)
             pre = jnp.dot(es[half], wc[...], preferred_element_type=F32) + bias
             th = jnp.tanh(pre)
             hs[half] = (jnp.maximum(pre, 0.0) - 0.5 * jnp.log(1.0 + jnp.abs(th))).astype(BF16)
-            ts[half] = ((1.0 + th) * jnp.dot(ds[half], wc[...], preferred_element_type=F32)).astype(BF16)
             filt = jnp.dot(hs[half], fc[...], preferred_element_type=F32)
-            dfilt = jnp.dot(ts[half], fc[...], preferred_element_type=F32)
+            if slope:
+                ts[half] = ((1.0 + th) * jnp.dot(ds[half], wc[...], preferred_element_type=F32)).astype(BF16)
+                dfilt = jnp.dot(ts[half], fc[...], preferred_element_type=F32)
             for a in range(SUB):
                 lane = half * SUB + a
                 fa = filt[a * blk:(a + 1) * blk, :]
-                da = dfilt[a * blk:(a + 1) * blk, :]
                 e = er[:, lane:lane + 1]
-                p = pr[:, lane:lane + 1]
-                gv = fa * e
-                msg_rows.append(jnp.sum(gv[:, 0:feat] * x0, axis=0, keepdims=True))
-                g1_s[k, first + lane] = gv[:, feat:2 * feat].astype(BF16)
-                dg_s[k, first + lane] = (da * (e * half_kappa) + fa * p).astype(BF16)
-        msg[0, k, pl.ds(pl.multiple_of(first, GROUP), GROUP), :] = jnp.concatenate(msg_rows, axis=0)
+                if forward:
+                    gv = fa * e
+                    msg_rows.append(jnp.sum(gv[:, 0:feat] * x0, axis=0, keepdims=True))
+                    g1_s[k, first + lane] = gv[:, feat:2 * feat].astype(BF16)
+                if slope:
+                    da = dfilt[a * blk:(a + 1) * blk, :]
+                    p = pr[:, lane:lane + 1]
+                    dg_s[k, first + lane] = (da * (e * half_kappa) + fa * p).astype(BF16)
+        if forward:
+            msg[0, k, pl.ds(pl.multiple_of(first, GROUP), GROUP), :] = jnp.concatenate(msg_rows, axis=0)
+
+    steps = blk // GROUP
+    late = slots - 1
+    parts = 4
+    cuts = [steps * p // parts for p in range(parts + 1)]
+
+    def late_slopes(part):
+        def late_step(step, carry):
+            filter_group(late, step, None, False, True)
+            return carry
+
+        lax.fori_loop(cuts[part], cuts[part + 1], late_step, 0)
+
+    to_sib = [[], []]
+
+    def send_message(layer, k):
+        to_sib[layer].append(send(msg.at[layer, k], sibmsg.at[layer, k], me_r, sib))
 
     for k in range(slots):
         x0 = xbuf[0][cols[k]]
 
         def filter_step(step, carry, k=k, x0=x0):
-            filter_group(k, step, x0)
+            filter_group(k, step, x0, True, k != late)
             return carry
 
-        lax.fori_loop(0, blk // GROUP, filter_step, 0)
-
-    def reduce_messages(layer):
-        to_sib = send(msg.at[layer], sibmsg.at[layer], me_r, sib)
+        lax.fori_loop(0, steps, filter_step, 0)
+        send_message(0, k)
+
+    def reduce_messages(layer, part):
         own_rows = posblk[...]
         sib_rows = rowpos[sib]
-        to_sib.wait_recv()
+        for copy in to_sib[layer]:
+            copy.wait_recv()
 
         def share(zz):
             dest = (zz * 2 + core).astype(F32)
@@ -192,6 +215,7 @@
             sbuf[layer, o] = share(zz)
             copies.append(send(sbuf.at[layer, o], rbuf.at[layer, o], me_r, zz * 2 + core))
         total = share(z)
+        late_slopes(part)
         for o, copy in enumerate(copies):
             copy.wait_recv()
             total = total + rbuf[layer, o]
@@ -213,10 +237,11 @@
         for copy in local:
             copy.wait_recv()
 
-    message = reduce_messages(0)
+    message = reduce_messages(0, 0)
     act, sig0 = ssp_parts(dot_nn(message, wu1[0]))
     features = features + dot_nn(act, wu2[0])
     x_copies = gather_features(1, dot_nn(features, w_in[1]))
+    late_slopes(1)
     for copy in x_copies:
         copy.wait_recv()
 
@@ -225,16 +250,17 @@
 
         def message_step(step, carry, k=k, x1=x1):
             first = step * GROUP
-            parts = [
+            lines = [
                 jnp.sum(g1_s[k, first + a].astype(F32) * x1, axis=0, keepdims=True)
                 for a in range(GROUP)
             ]
-            msg[1, k, pl.ds(pl.multiple_of(first, GROUP), GROUP), :] = jnp.concatenate(parts, axis=0)
+            msg[1, k, pl.ds(pl.multiple_of(first, GROUP), GROUP), :] = jnp.concatenate(lines, axis=0)
             return carry
 
-        lax.fori_loop(0, blk // GROUP, message_step, 0)
-
-    message = reduce_messages(1)
+        lax.fori_loop(0, steps, message_step, 0)
+        send_message(1, k)
+
+    message = reduce_messages(1, 2)
     act, sig1 = ssp_parts(dot_nn(message, wu1[1]))
     features = features + dot_nn(act, wu2[1])
 
@@ -244,6 +270,7 @@
 
     grad_msg = dot_nt(dot_nt(grad_feat, wu2[1]) * sig1, wu1[1])
     across, local = gather_cotangents(1, grad_msg)
+    late_slopes(3)
     finish_cotangents(1, across, local)
 
     for k in range(slots):
@@ -340,7 +367,7 @@
     n_gauss = rbf_weight.shape[1]
     nz = n_col // 2
     n_sems = (
-        (n_col - 1 + n_row - 1) * 2 + 2 * (n_row - 1) + 2 * (1 + nz - 1)
+        (n_col - 1 + n_row - 1) * 2 + 2 * (n_row - 1) + 2 * (slots + nz - 1)
         + 2 * (2 * nz - 1) + (n_row - 1)
     )
     vm = pltpu.VMEM

time: 116 us -> 113 us (0.974)
  Pallas kernels: 112 us -> 109 us
    pallas_call x1, Pallas kernels: 112 us -> 109 us  [body(): pl.pallas_call(partial(kernel, n_row, n_col, slots), out_shape=(jax.Shape...]
where the time goes in v1:
time: 113 us; the launch traced here: 112 us
  Pallas kernels  109 us (96%)
  local copies, waits for them, and re-layouts  3.14 us (3%)
    pallas_call x1, Pallas kernels, body(): pl.pallas_call(partial(kernel, n_row, n_col, slots), out_shape=(jax.Shape...  109 us
    unnamed x7, local copies, waits for them, and re-layouts  3.14 us

profile of v1, /device:TPU:0, one launch (start us, length us, event | category | flops | bytes accessed | tf_op | source)
XLA Modules:
  0.0 112.4 jit_solution(12370022096152820385)
XLA Ops:
  0.6 1.5 %copy.15.wo1 = f32[128,64]{1,0:T(8,128)} copy(f32[128,64]{0,1:T(8,128)} %param.24) | data formatting | bytes 65536 | tf_op args[11]
  2.1 108.6 %shard_map.140 = (f32[1,128]{1,0:T(1,128)}, f32[3,128]{1,0:T(4,128)}) custom-call(s32[1,1,2,3]{3,2,1,0:T(2,128)} %tl.1, f32[3,128]{1,0:T(4,128)} %pos.1, s32[1,128]{1,0:T(1,128)} %bitcast.3, s32[1,1,2,128,128]{4,3,2,1,0:T(8,128)} %mask.1, f32[100,128]{1,0:T(8,128)} %embed.1, f32[2,128,128]{2,1,0:T(8,128)} %w_in.1, bf16[2,256,128]{2,1,0:T(8,128)(2,1)} %rbf_w.1, ...), custom_call_target="tpu_custom_call" | custom-call | tf_op jit(solution)/shard_map/pallas_call | solution.py:395
  110.7 0.0 copy-start.1
  110.7 0.0 copy-start
  110.7 0.6 copy-done.1
  111.3 0.5 copy.18
  111.8 0.0 copy-done
  111.8 0.6 copy.19
Async XLA Ops:
  110.7 0.6 copy-start.1
  110.7 1.1 copy-start

commit v2 on v1

--- a/solution.py
+++ b/solution.py
@@ -12,7 +12,7 @@
 NORM_DIV = 4.0
 HIGH = lax.Precision.HIGHEST
 MESH = pl.DeviceIdType.MESH
-GROUP = 8
+GROUP = 16
 SUB = 4
 F32 = jnp.float32
 BF16 = jnp.bfloat16
@@ -101,9 +101,9 @@
     bias = 0.5 * jnp.concatenate([rbf_b[0:1, :], rbf_b[1:2, :]], axis=1)
 
     sharp = (n_gauss / CUTOFF) ** 2 / 32.0
-    alpha = math.sqrt(sharp / math.log(2.0))
+    alpha = math.sqrt(sharp)
     centers = lax.broadcasted_iota(jnp.int32, (1, n_gauss), 1).astype(F32) * (alpha * CUTOFF / n_gauss)
-    half_kappa = -math.log(2.0) * alpha
+    half_kappa = -alpha
 
     for copy in pos_copies:
         copy.wait_recv()
@@ -142,7 +142,7 @@
             for a in range(SUB):
                 lane = half * SUB + a
                 t = ur[:, lane:lane + 1] - centers
-                e = jnp.exp2(-(t * t))
+                e = jnp.exp(-(t * t))
                 es[half, a * blk:(a + 1) * blk, :] = e.astype(BF16)
                 if slope:
                     ds[half, a * blk:(a + 1) * blk, :] = (t * e).astype(BF16)

time: 113 us -> 109 us (0.965)
  Pallas kernels: 109 us -> 105 us
    pallas_call x1, Pallas kernels: 109 us -> 105 us  [body(): pl.pallas_call(partial(kernel, n_row, n_col, slots), out_shape=(jax.Shape...]
where the time goes in v2:
time: 109 us
  Pallas kernels  105 us (96%)
  local copies, waits for them, and re-layouts  3.14 us (3%)
    pallas_call x1, Pallas kernels, body(): pl.pallas_call(partial(kernel, n_row, n_col, slots), out_shape=(jax.Shape...  105 us
    unnamed x7, local copies, waits for them, and re-layouts  3.14 us

profile of v2, /device:TPU:0, one launch (start us, length us, event | category | flops | bytes accessed | tf_op | source)
XLA Modules:
  0.0 108.6 jit_solution(15615790991285686365)
XLA Ops:
  0.6 1.5 %copy.15.wo1 = f32[128,64]{1,0:T(8,128)} copy(f32[128,64]{0,1:T(8,128)} %param.24) | data formatting | bytes 65536 | tf_op args[11]
  2.1 104.8 %shard_map.140 = (f32[1,128]{1,0:T(1,128)}, f32[3,128]{1,0:T(4,128)}) custom-call(s32[1,1,2,3]{3,2,1,0:T(2,128)} %tl.1, f32[3,128]{1,0:T(4,128)} %pos.1, s32[1,128]{1,0:T(1,128)} %bitcast.3, s32[1,1,2,128,128]{4,3,2,1,0:T(8,128)} %mask.1, f32[100,128]{1,0:T(8,128)} %embed.1, f32[2,128,128]{2,1,0:T(8,128)} %w_in.1, bf16[2,256,128]{2,1,0:T(8,128)(2,1)} %rbf_w.1, ...), custom_call_target="tpu_custom_call" | custom-call | tf_op jit(solution)/shard_map/pallas_call | solution.py:395
  106.9 0.0 copy-start.1
  106.9 0.0 copy-start
  107.0 0.6 copy-done.1
  107.5 0.5 copy.18
  108.0 0.0 copy-done
  108.1 0.6 copy.19
Async XLA Ops:
  106.9 0.6 copy-start.1
  106.9 1.1 %copy-start = (f32[3,128]{1,0:T(4,128)S(1)}, f32[3,128]{1,0:T(4,128)}, u32[]{:S(2)}) copy-start(f32[3,128]{1,0:T(4,128)} %get-tuple-element.9) | copy-start | bytes 4612
